TPU v7x, 512 devices: a whole 4x8x8 slice. The times are simulated.
512 devices in a mesh: row: 32 (over z, x_hi, core), col: 16 (over x_lo, y).
Axes of the slice: x: 4 (x_hi: 2, x_lo: 2; x = x_hi * 2 + x_lo), y: 8, z: 8, core: 2. Of those that a mesh axis runs over, the one named last changes fastest.
Arguments:
- trunk_in: bfloat16 [1536, 32768], P('col', 'row'), may hold values from -24 to 24
- conv_weight: bfloat16 [5, 1536, 1536], P(None, 'col'), may hold values from -0.0625 to 0.0625
- conv_bias: float32 [1536], P('col'), may hold values from -3 to 3
- norm_gain: float32 [1536], replicated, may hold values from 0.1 to 1.9
- pair_proj: bfloat16 [64, 1536], replicated, may hold values from -0.15625 to 0.15625
- pair_in: bfloat16 [2048, 512, 128], P('row', 'col'), may hold values from -6 to 6
- opm_weight: bfloat16 [1024, 128], replicated, may hold values from -0.1875 to 0.1875
- pair_bias: float32 [128], replicated, may hold values from -3 to 3
Outputs:
- trunk_out: bfloat16 [1536, 32768], P('col', 'row')
- pair_out: bfloat16 [2048, 512, 128], P('row', 'col')
All inputs are finite; a program needn't handle non-finite values.
Results may differ from a plain program's by a relative error of at most 0.012.
Values may be sent and summed in bfloat16 or wider, within the bound.
A program may use at most 64 MiB of HBM per device.

v0:
```python
import jax
import jax.numpy as jnp
from jax import lax
from jax.sharding import PartitionSpec as P

TRUNK_CHANNELS = 1536
DILATION_STEP = 8
POOL = 16
OPM = 32
WINDOWS = 4
EPSILON = 1e-05


def with_halo(cells, sides, width):
    for axis, dim in sides:
        count = lax.axis_size(axis)
        ends = count - 1
        head = lax.slice_in_dim(cells, 0, width, axis=dim)
        tail = lax.slice_in_dim(cells, cells.shape[dim] - width, cells.shape[dim], axis=dim)
        cells = jnp.concatenate(
            [
                lax.ppermute(tail, axis, [(i, (i + 1) % count) for i in range(ends)]),
                cells,
                lax.ppermute(head, axis, [((i + 1) % count, i) for i in range(ends)]),
            ],
            axis=dim,
        )
    return cells


def partner_2(block, axis, bit):
    count = lax.axis_size(axis)
    route = []
    for low in range(count):
        high = low | 1 << bit
        if high != low and high < count:
            route += [(low, high), (high, low)]
    return lax.ppermute(block, axis, route)


def per_device(
    trunk_in, conv_weight, conv_bias, norm_gain, pair_proj, pair_in, opm_weight, pair_bias
):
    local_channels = trunk_in.shape[0]
    token_positions = trunk_in.shape[1]
    kernel = conv_weight.shape[0]
    border_width = 2 * DILATION_STEP
    per_window = lax.axis_size("row") // WINDOWS
    row_index = lax.axis_index("row")
    col_index = lax.axis_index("col")
    in_window = row_index % per_window
    source = trunk_in.astype(jnp.float32)
    zero_sum = jnp.zeros((local_channels, token_positions), jnp.float32)
    gathered = lax.all_gather(trunk_in, "col", axis=0, tiled=True)
    padded_trunk = with_halo(gathered, (("row", 1),), border_width)
    values = padded_trunk.astype(jnp.float32)
    scale = lax.rsqrt(jnp.mean(values * values, axis=0, keepdims=True) + EPSILON)
    gelu_output = jax.nn.gelu(values * norm_gain[:, None] * scale).astype(jnp.bfloat16)
    conv_sum = zero_sum
    for tap_offset in range(kernel):
        conv_sum = conv_sum + jnp.dot(
            conv_weight[tap_offset],
            gelu_output[
                :, tap_offset * DILATION_STEP : tap_offset * DILATION_STEP + token_positions
            ],
            preferred_element_type=jnp.float32,
        )
    trunk_out = (source + conv_sum + conv_bias[:, None]).astype(jnp.bfloat16)
    pooled = (
        trunk_out.astype(jnp.float32)
        .reshape(local_channels, token_positions // POOL, POOL)
        .mean(axis=2)
        .astype(jnp.bfloat16)
    )
    own_proj = lax.dynamic_slice_in_dim(pair_proj, col_index * local_channels, local_channels, 1)
    pooled_f = pooled.astype(jnp.float32)
    partial_proj = lax.dot_general(
        pooled, own_proj, (((0,), (1,)), ((), ())), preferred_element_type=jnp.float32
    )
    projected, sums = lax.psum((partial_proj, jnp.sum(pooled_f * pooled_f, axis=0)), "col")
    sides = (projected * lax.rsqrt(sums / TRUNK_CHANNELS + EPSILON)[:, None]).astype(jnp.bfloat16)
    row_side = sides[:, :OPM]
    collected = sides[:, OPM:]
    col_block = pair_in.shape[1]
    pooled_rows = row_side.shape[0]
    for bit_num in range(per_window.bit_length() - 1):
        partner = partner_2(collected, "row", bit_num)
        upper_half = in_window // 2**bit_num % 2 == 1
        collected = jnp.where(
            upper_half,
            jnp.concatenate([partner, collected], axis=0),
            jnp.concatenate([collected, partner], axis=0),
        )
    own_cols = lax.dynamic_slice_in_dim(collected, col_index * col_block, col_block, 0)
    outer = (
        row_side.astype(jnp.float32)[:, None, :, None]
        * own_cols.astype(jnp.float32)[None, :, None, :]
    ).astype(jnp.bfloat16)
    outer = outer.reshape(pooled_rows * col_block, OPM * OPM)
    update = jnp.dot(outer, opm_weight, preferred_element_type=jnp.float32).reshape(pair_in.shape)
    pair_out = (pair_in.astype(jnp.float32) + update + pair_bias).astype(jnp.bfloat16)
    return (trunk_out, pair_out)


def solution(mesh):
    return jax.shard_map(
        per_device,
        mesh=mesh,
        in_specs=(
            P("col", "row"),
            P(None, "col", None),
            P("col"),
            P(),
            P(),
            P("row", "col", None),
            P(),
            P(),
        ),
        out_specs=(P("col", "row"), P("row", "col", None)),
        check_vma=False,
    )
```

profile of v0, /device:TPU:64, one launch (start us, length us, event | category | flops | bytes accessed | tf_op | source)
XLA Modules:
  0.0 214.4 jit_solution(7731478625536114508)
XLA Ops:
  7.2 0.7 all-gather.2.cloned.1.call-update
  7.9 83.4 %all-gather.2.cloned.1.call-done = bf16[1536,1024]{1,0:T(8,128)(2,1)} async-done(((bf16[96,1024]{1,0:T(8,128)(2,1)}), bf16[1536,1024]{1,0:T(8,128)(2,1)}) %all-gather.2.cloned.1.call-update) | async-done | bytes 3145744 | tf_op jit(solution)/shard_map/all_gather | solution.py:54
  91.3 1.3 fusion.69
  92.6 1.9 collective-permute-start
  94.5 6.0 %collective-permute-start.1 = (bf16[1536,16]{1,0:T(8,128)(2,1)S(1)}, bf16[1536,16]{1,0:T(8,128)(2,1)S(1)}, u32[]{:S(2)}, u32[]{:S(2)}) collective-permute-start(bf16[1536,16]{1,0:T(8,128)(2,1)S(1)} %get-tuple-element.4), channel_id=1, source_target_pairs={{16,0},{32,16},{48,32},{64,48},{80,64},{96,80},{112,96},{128,112},... | collective-permute-start | bytes 147464 | tf_op jit(solution)/shard_map/ppermute | solution.py:24
  100.6 3.5 %collective-permute-done = bf16[1536,16]{1,0:T(8,128)(2,1)S(1)} collective-permute-done((bf16[1536,16]{1,0:T(8,128)(2,1)S(1)}, bf16[1536,16]{1,0:T(8,128)(2,1)S(1)}, u32[]{:S(2)}, u32[]{:S(2)}) %collective-permute-start) | collective-permute-done | bytes 49184 | tf_op jit(solution)/shard_map/ppermute | solution.py:22
  104.1 1.7 collective-permute-done.1
  105.9 7.5 %concatenate.21 = bf16[1536,1056]{1,0:T(8,128)(2,1)} concatenate(bf16[1536,16]{1,0:T(8,128)(2,1)S(1)} %collective-permute-done, bf16[1536,1024]{1,0:T(8,128)(2,1)} %all-gather.2.cloned.1.call-done, bf16[1536,16]{1,0:T(8,128)(2,1)S(1)} %collective-permute-done.1), dimensions={1} | concatenate | bytes 6488064 | tf_op jit(solution)/shard_map/concatenate | solution.py:20
  113.4 2.9 %fusion.8 = f32[1056]{0:T(1024)S(1)} fusion(bf16[1536,1056]{1,0:T(8,128)(2,1)} %concatenate.21), kind=kLoop, calls=%fused_computation.12 | loop fusion | flops 4864992 | bytes 3248256 | tf_op jit(solution)/shard_map/reduce_sum | solution.py:57
  116.3 0.1 copy-done.1
  116.4 3.7 %fusion.3 = bf16[1536,1056]{1,0:T(8,128)(2,1)S(1)} fusion(bf16[1536,1056]{1,0:T(8,128)(2,1)S(1)} %copy-done.1, f32[1056]{0:T(1024)S(1)} %add_rsqrt_fusion, f32[1536]{0:T(1024)S(1)} %copy-done.5), kind=kLoop, calls=%fused_computation.7 | loop fusion | flops 19464192 | bytes 6498432 | tf_op jit(solution)/shard_map/convert_element_type | solution.py:58
  120.1 1.1 fusion.13
  121.3 1.1 fusion.15
  122.4 1.1 fusion.17
  123.6 1.1 fusion.19
  124.8 0.7 fusion.47
  125.5 0.1 copy.21
  125.6 0.1 bitcast_reduce_fusion
  125.7 0.1 multiply_reduce_fusion
  125.8 1.0 fusion.61
  126.8 62.4 %all-reduce = (f32[64,64]{0,1:T(8,128)S(1)}, f32[64]{0:T(128)S(1)}) all-reduce(f32[64,64]{0,1:T(8,128)S(1)} %fusion.61, f32[64]{0:T(128)S(1)} %multiply_reduce_fusion), channel_id=1, replica_groups=mesh['row'=32,'col'=16] {'col'}, use_global_device_ids=true, to_apply=%region_2.3 | all-reduce | flops 4160 | bytes 33280 | tf_op jit(solution)/shard_map/psum | solution.py:80
  189.2 1.9 collective-permute-start.2
  191.2 1.1 collective-permute-done.2
  192.3 0.1 maximum_select_fusion.1
  192.3 4.5 %collective-permute-start.3 = (bf16[128,32]{0,1:T(8,128)(2,1)S(1)}, bf16[128,32]{0,1:T(8,128)(2,1)S(1)}, u32[]{:S(2)}, u32[]{:S(2)}) collective-permute-start(bf16[128,32]{0,1:T(8,128)(2,1)S(1)} %maximum_select_fusion.1), channel_id=1, source_target_pairs={{0,32},{32,0},{16,48},{48,16},{64,96},{96,64},{80,112},{112,80},{1... | collective-permute-start | bytes 24584 | tf_op jit(solution)/shard_map/ppermute | solution.py:38
  196.9 2.5 %collective-permute-done.3 = bf16[128,32]{0,1:T(8,128)(2,1)S(1)} collective-permute-done((bf16[128,32]{0,1:T(8,128)(2,1)S(1)}, bf16[128,32]{0,1:T(8,128)(2,1)S(1)}, u32[]{:S(2)}, u32[]{:S(2)}) %collective-permute-start.3) | collective-permute-done | bytes 8224 | tf_op jit(solution)/shard_map/ppermute | solution.py:38
  199.4 1.9 collective-permute-start.4
  201.4 0.2 copy.23
  201.6 3.4 %collective-permute-done.4 = bf16[256,32]{0,1:T(8,128)(2,1)S(1)} collective-permute-done((bf16[256,32]{0,1:T(8,128)(2,1)S(1)}, bf16[256,32]{0,1:T(8,128)(2,1)S(1)}, u32[]{:S(2)}, u32[]{:S(2)}) %collective-permute-start.4) | collective-permute-done | bytes 16416 | tf_op jit(solution)/shard_map/ppermute | solution.py:38
  205.0 0.1 fusion.65
  205.2 0.2 mul.101
  205.5 2.1 fusion.25
  (26 shorter events, 0.3 us)
Async XLA Ops:
  7.2 198.3 %copy-start = (bf16[1024,128]{1,0:T(8,128)(2,1)S(1)}, bf16[1024,128]{1,0:T(8,128)(2,1)}, u32[]{:S(2)}) copy-start(bf16[1024,128]{1,0:T(8,128)(2,1)} %param.14) | copy-start | bytes 786436
  7.2 84.1 %all-gather.2.cloned.1.call-start = ((), (), s32[]{:S(2)}) async-start(), calls=%async_computation | async-start | bytes 3342336 | tf_op jit(solution)/shard_map/all_gather | solution.py:54
  92.6 11.5 %collective-permute-start = (bf16[1536,16]{1,0:T(8,128)(2,1)S(1)}, bf16[1536,16]{1,0:T(8,128)(2,1)S(1)}, u32[]{:S(2)}, u32[]{:S(2)}) collective-permute-start(bf16[1536,16]{1,0:T(8,128)(2,1)S(1)} %get-tuple-element.5), channel_id=1, source_target_pairs={{0,16},{16,32},{32,48},{48,64},{64,80},{80,96},{96,112},{112,128},... | collective-permute-start | bytes 147464 | tf_op jit(solution)/shard_map/ppermute | solution.py:22
  94.5 11.3 %collective-permute-start.1 = (bf16[1536,16]{1,0:T(8,128)(2,1)S(1)}, bf16[1536,16]{1,0:T(8,128)(2,1)S(1)}, u32[]{:S(2)}, u32[]{:S(2)}) collective-permute-start(bf16[1536,16]{1,0:T(8,128)(2,1)S(1)} %get-tuple-element.4), channel_id=1, source_target_pairs={{16,0},{32,16},{48,32},{64,48},{80,64},{96,80},{112,96},{128,112},... | collective-permute-start | bytes 147464 | tf_op jit(solution)/shard_map/ppermute | solution.py:24
  113.3 3.1 %copy-start.1 = (bf16[1536,1056]{1,0:T(8,128)(2,1)S(1)}, bf16[1536,1056]{1,0:T(8,128)(2,1)}, u32[]{:S(2)}) copy-start(bf16[1536,1056]{1,0:T(8,128)(2,1)} %concatenate.21) | copy-start | bytes 9732100
  113.3 3.1 %copy-start.5 = (f32[1536]{0:T(1024)S(1)}, f32[1536]{0:T(1024)}, u32[]{:S(2)}) copy-start(f32[1536]{0:T(1024)} %param.11) | copy-start | bytes 18436
  116.4 3.7 %copy-start.4 = (bf16[5,96,1536]{2,1,0:T(8,128)(2,1)S(1)}, bf16[5,96,1536]{2,1,0:T(8,128)(2,1)}, u32[]{:S(2)}) copy-start(bf16[5,96,1536]{2,1,0:T(8,128)(2,1)} %param.9) | copy-start | bytes 4423684
  122.4 2.3 %copy-start.2 = (bf16[96,1024]{1,0:T(8,128)(2,1)S(1)}, bf16[96,1024]{1,0:T(8,128)(2,1)}, u32[]{:S(2)}) copy-start(bf16[96,1024]{1,0:T(8,128)(2,1)} %param.8) | copy-start | bytes 589828
  122.4 2.3 %copy-start.6 = (f32[96]{0:T(128)S(1)}, f32[96]{0:T(128)}, u32[]{:S(2)}) copy-start(f32[96]{0:T(128)} %param.10) | copy-start | bytes 1156
  124.7 80.7 %copy-start.7 = (bf16[64,32,128]{2,1,0:T(8,128)(2,1)S(1)}, bf16[64,32,128]{2,1,0:T(8,128)(2,1)}, u32[]{:S(2)}) copy-start(bf16[64,32,128]{2,1,0:T(8,128)(2,1)} %param.13) | copy-start | bytes 1572868
  124.7 80.7 %copy-start.8 = (f32[128]{0:T(128)S(1)}, f32[128]{0:T(128)}, u32[]{:S(2)}) copy-start(f32[128]{0:T(128)} %param.15) | copy-start | bytes 1540
  125.5 82.1 %copy-start.3 = (bf16[96,1024]{1,0:T(8,128)(2,1)}, bf16[96,1024]{1,0:T(8,128)(2,1)S(1)}, u32[]{:S(2)}) copy-start(bf16[96,1024]{1,0:T(8,128)(2,1)S(1)} %fusion.47) | copy-start | bytes 589828
  189.2 3.1 %collective-permute-start.2 = (bf16[64,32]{0,1:T(8,128)(2,1)S(1)}, bf16[64,32]{0,1:T(8,128)(2,1)S(1)}, u32[]{:S(2)}, u32[]{:S(2)}) collective-permute-start(bf16[64,32]{0,1:T(8,128)(2,1)S(1)} %get-tuple-element.7), channel_id=1, source_target_pairs={{0,16},{16,0},{32,48},{48,32},{64,80},{80,64},{96,112},{112,96},{1... | collective-permute-start | bytes 12296 | tf_op jit(solution)/shard_map/ppermute | solution.py:38
  192.3 7.0 %collective-permute-start.3 = (bf16[128,32]{0,1:T(8,128)(2,1)S(1)}, bf16[128,32]{0,1:T(8,128)(2,1)S(1)}, u32[]{:S(2)}, u32[]{:S(2)}) collective-permute-start(bf16[128,32]{0,1:T(8,128)(2,1)S(1)} %maximum_select_fusion.1), channel_id=1, source_target_pairs={{0,32},{32,0},{16,48},{48,16},{64,96},{96,64},{80,112},{112,80},{1... | collective-permute-start | bytes 24584 | tf_op jit(solution)/shard_map/ppermute | solution.py:38
  199.4 5.6 %collective-permute-start.4 = (bf16[256,32]{0,1:T(8,128)(2,1)S(1)}, bf16[256,32]{0,1:T(8,128)(2,1)S(1)}, u32[]{:S(2)}, u32[]{:S(2)}) collective-permute-start(bf16[256,32]{0,1:T(8,128)(2,1)S(1)} %maximum_select_fusion), channel_id=1, source_target_pairs={{0,64},{64,0},{16,80},{80,16},{32,96},{96,32},{48,112},{112,48},{1... | collective-permute-start | bytes 49160 | tf_op jit(solution)/shard_map/ppermute | solution.py:38
Sparse Core Ops, SparseCore 0:
  10.1 81.1 all-gather.1
where the time goes:
time: 215 us; the launch traced here: 214 us
  waiting for transfers between devices  96.4 us (45%)
  blocking collectives  62.4 us (29%)
  starting transfers between devices  16.3 us (8%)
  between operations  14.4 us (7%)
  local copies, waits for them, and re-layouts  9.64 us (4%)
  matrix products  8.25 us (4%)
  other arithmetic  7.03 us (3%)
    all_gather x1, waiting for transfers between devices, per_device(): gathered = lax.all_gather(trunk_in, 'col', axis=0, tiled=True)  83.4 us
    psum x1, blocking collectives, per_device(): lax.psum((partial_proj, jnp.sum(pooled_f * pooled_f, axis=0)), 'col')  62.4 us
    ppermute x3, starting transfers between devices, partner_2(): return lax.ppermute(block, axis, route)  8.33 us
    concatenate x1, local copies, waits for them, and re-layouts, with_halo(): jnp.concatenate([lax.ppermute(tail, axis, [(i, (i + 1) % count) for i in...  7.49 us
    ppermute x3, waiting for transfers between devices, partner_2(): return lax.ppermute(block, axis, route)  7.02 us
    ppermute x1, starting transfers between devices, with_halo(): lax.ppermute(head, axis, [((i + 1) % count, i) for i in range(ends)])  6.05 us
    dot_general x5, matrix products, per_device(): jnp.dot(conv_weight[tap_offset], gelu_output[:, tap_offset * DILATION_STE...  5.25 us
  transfers between devices with their start and end apart: 6, of which 6 were waited for; matrix products, arithmetic and copies ran while one was open for 0% of the time, Pallas kernels for 0%

commit v1 on v0

--- a/solution.py
+++ b/solution.py
@@ -51,7 +51,8 @@
     in_window = row_index % per_window
     source = trunk_in.astype(jnp.float32)
     zero_sum = jnp.zeros((local_channels, token_positions), jnp.float32)
-    gathered = lax.all_gather(trunk_in, "col", axis=0, tiled=True)
+    repeated = jnp.stack([trunk_in] * lax.axis_size("col"))
+    gathered = jnp.concatenate(lax.all_to_all(repeated, "col", 0, 0), axis=0)
     padded_trunk = with_halo(gathered, (("row", 1),), border_width)
     values = padded_trunk.astype(jnp.float32)
     scale = lax.rsqrt(jnp.mean(values * values, axis=0, keepdims=True) + EPSILON)

time: 215 us -> 200 us (0.930)
  the two profiles are of different devices: /device:TPU:64 before, /device:TPU:256 now
where the time goes in v1:
time: 200 us; the launch traced here: 199 us
  blocking collectives  142 us (71%)
  starting transfers between devices  17.7 us (9%)
  waiting for transfers between devices  12.4 us (6%)
  local copies, waits for them, and re-layouts  10 us (5%)
  matrix products  8.27 us (4%)
  other arithmetic  7.01 us (4%)
    all_to_all x1, blocking collectives, per_device(): gathered = jnp.concatenate(lax.all_to_all(repeated, 'col', 0, 0), axis=0)  79.8 us
    psum x1, blocking collectives, per_device(): lax.psum((partial_proj, jnp.sum(pooled_f * pooled_f, axis=0)), 'col')  62.5 us
    ppermute x3, starting transfers between devices, partner_2(): return lax.ppermute(block, axis, route)  8.55 us
    ppermute x1, starting transfers between devices, with_halo(): lax.ppermute(head, axis, [((i + 1) % count, i) for i in range(ends)])  7.26 us
    ppermute x3, waiting for transfers between devices, partner_2(): return lax.ppermute(block, axis, route)  6.8 us
    concatenate x1, local copies, waits for them, and re-layouts, with_halo(): jnp.concatenate([lax.ppermute(tail, axis, [(i, (i + 1) % count) for i in...  6.72 us
    dot_general x5, matrix products, per_device(): jnp.dot(conv_weight[tap_offset], gelu_output[:, tap_offset * DILATION_STE...  5.26 us
  transfers between devices with their start and end apart: 5, of which 5 were waited for; matrix products, arithmetic and copies ran while one was open for 0% of the time, Pallas kernels for 0%

profile of v1, /device:TPU:256, one launch (start us, length us, event | category | flops | bytes accessed | tf_op | source)
XLA Modules:
  0.0 198.7 jit_solution(9955061636600635783)
XLA Ops:
  0.6 1.4 stack.2
  2.0 79.8 %all_to_all.5 = bf16[16,96,1024]{2,1,0:T(8,128)(2,1)S(1)} all-to-all(bf16[16,96,1024]{2,1,0:T(8,128)(2,1)S(1)} %stack.2), channel_id=1, replica_groups=mesh['row'=32,'col'=16] {'col'}, dimensions={0} | all-to-all | bytes 6291456 | tf_op jit(solution)/shard_map/all_to_all | solution.py:55
  81.8 1.1 fusion.69
  82.9 1.9 collective-permute-start
  84.8 7.3 %collective-permute-start.1 = (bf16[1536,16]{1,0:T(8,128)(2,1)}, bf16[1536,16]{1,0:T(8,128)(2,1)}, u32[]{:S(2)}, u32[]{:S(2)}) collective-permute-start(bf16[1536,16]{1,0:T(8,128)(2,1)} %get-tuple-element.4), channel_id=1, source_target_pairs={{16,0},{32,16},{48,32},{64,48},{80,64},{96,80},{112,96},{128,112},... | collective-permute-start | bytes 147464 | tf_op jit(solution)/shard_map/ppermute | solution.py:24
  92.1 3.9 %collective-permute-done = bf16[1536,16]{1,0:T(8,128)(2,1)} collective-permute-done((bf16[1536,16]{1,0:T(8,128)(2,1)}, bf16[1536,16]{1,0:T(8,128)(2,1)}, u32[]{:S(2)}, u32[]{:S(2)}) %collective-permute-start) | collective-permute-done | bytes 49184 | tf_op jit(solution)/shard_map/ppermute | solution.py:22
  96.0 1.7 collective-permute-done.1
  97.7 6.7 %concatenate.21 = bf16[1536,1056]{1,0:T(8,128)(2,1)} concatenate(bf16[1536,16]{1,0:T(8,128)(2,1)} %collective-permute-done, bf16[1536,1024]{1,0:T(8,128)(2,1)S(1)} %bitcast.31, bf16[1536,16]{1,0:T(8,128)(2,1)} %collective-permute-done.1), dimensions={1} | concatenate | bytes 6488064 | tf_op jit(solution)/shard_map/concatenate | solution.py:20
  104.4 2.9 %fusion.8 = f32[1056]{0:T(1024)S(1)} fusion(bf16[1536,1056]{1,0:T(8,128)(2,1)} %concatenate.21), kind=kLoop, calls=%fused_computation.12 | loop fusion | flops 4864992 | bytes 3248256 | tf_op jit(solution)/shard_map/reduce_sum | solution.py:58
  107.3 0.1 copy-done.1
  107.5 3.7 %fusion.3 = bf16[1536,1056]{1,0:T(8,128)(2,1)S(1)} fusion(bf16[1536,1056]{1,0:T(8,128)(2,1)S(1)} %copy-done.1, f32[1056]{0:T(1024)S(1)} %add_rsqrt_fusion, f32[1536]{0:T(1024)S(1)} %copy-done.5), kind=kLoop, calls=%fused_computation.7 | loop fusion | flops 19464192 | bytes 6498432 | tf_op jit(solution)/shard_map/convert_element_type | solution.py:59
  111.1 1.1 fusion.13
  112.3 1.1 fusion.15
  113.5 1.1 fusion.17
  114.6 1.1 fusion.19
  115.8 0.7 fusion.47
  116.5 0.1 copy.40
  116.7 0.1 bitcast_reduce_fusion
  116.8 0.1 multiply_reduce_fusion
  116.9 1.0 fusion.61
  117.8 62.5 %all-reduce = (f32[64,64]{0,1:T(8,128)S(1)}, f32[64]{0:T(128)S(1)}) all-reduce(f32[64,64]{0,1:T(8,128)S(1)} %fusion.61, f32[64]{0:T(128)S(1)} %multiply_reduce_fusion), channel_id=1, replica_groups=mesh['row'=32,'col'=16] {'col'}, use_global_device_ids=true, to_apply=%region_2.3 | all-reduce | flops 4160 | bytes 33280 | tf_op jit(solution)/shard_map/psum | solution.py:81
  180.4 1.9 collective-permute-start.2
  182.3 1.1 collective-permute-done.2
  183.4 0.1 maximum_select_fusion.1
  183.5 4.5 %collective-permute-start.3 = (bf16[128,32]{0,1:T(8,128)(2,1)S(1)}, bf16[128,32]{0,1:T(8,128)(2,1)S(1)}, u32[]{:S(2)}, u32[]{:S(2)}) collective-permute-start(bf16[128,32]{0,1:T(8,128)(2,1)S(1)} %maximum_select_fusion.1), channel_id=1, source_target_pairs={{0,32},{32,0},{16,48},{48,16},{64,96},{96,64},{80,112},{112,80},{1... | collective-permute-start | bytes 24584 | tf_op jit(solution)/shard_map/ppermute | solution.py:38
  188.0 2.5 %collective-permute-done.3 = bf16[128,32]{0,1:T(8,128)(2,1)S(1)} collective-permute-done((bf16[128,32]{0,1:T(8,128)(2,1)S(1)}, bf16[128,32]{0,1:T(8,128)(2,1)S(1)}, u32[]{:S(2)}, u32[]{:S(2)}) %collective-permute-start.3) | collective-permute-done | bytes 8224 | tf_op jit(solution)/shard_map/ppermute | solution.py:38
  190.6 2.2 %collective-permute-start.4 = (bf16[256,32]{0,1:T(8,128)(2,1)S(1)}, bf16[256,32]{0,1:T(8,128)(2,1)S(1)}, u32[]{:S(2)}, u32[]{:S(2)}) collective-permute-start(bf16[256,32]{0,1:T(8,128)(2,1)S(1)} %maximum_select_fusion), channel_id=1, source_target_pairs={{0,64},{64,0},{16,80},{80,16},{32,96},{96,32},{48,112},{112,48},{1... | collective-permute-start | bytes 49160 | tf_op jit(solution)/shard_map/ppermute | solution.py:38
  192.8 0.2 copy.42
  193.0 3.2 %collective-permute-done.4 = bf16[256,32]{0,1:T(8,128)(2,1)S(1)} collective-permute-done((bf16[256,32]{0,1:T(8,128)(2,1)S(1)}, bf16[256,32]{0,1:T(8,128)(2,1)S(1)}, u32[]{:S(2)}, u32[]{:S(2)}) %collective-permute-start.4) | collective-permute-done | bytes 16416 | tf_op jit(solution)/shard_map/ppermute | solution.py:38
  196.2 0.1 fusion.65
  196.4 0.2 mul.101
  196.7 2.1 %fusion.25 = bf16[64,32,128]{2,1,0:T(8,128)(2,1)} fusion(f32[32,1024]{1,0:T(8,128)S(1)} %mul.101, f32[64,1024]{1,0:T(8,128)S(1)} %copy.42, bf16[64,32,128]{2,1,0:T(8,128)(2,1)S(1)} %copy-done.7, f32[128]{0:T(128)S(1)} %copy-done.8, bf16[1024,128]{1,0:T(8,128)(2,1)S(1)} %copy-done), kind=kOutput, calls=%fused_computation.29 | convolution fusion | flops 542113792 | bytes 1704448 | tf_op jit(solution)/shard_map/dot_general | solution.py:101
  (25 shorter events, 0.2 us)
Async XLA Ops:
  0.6 196.0 %copy-start = (bf16[1024,128]{1,0:T(8,128)(2,1)S(1)}, bf16[1024,128]{1,0:T(8,128)(2,1)}, u32[]{:S(2)}) copy-start(bf16[1024,128]{1,0:T(8,128)(2,1)} %param.14) | copy-start | bytes 786436
  82.9 13.1 %collective-permute-start = (bf16[1536,16]{1,0:T(8,128)(2,1)}, bf16[1536,16]{1,0:T(8,128)(2,1)}, u32[]{:S(2)}, u32[]{:S(2)}) collective-permute-start(bf16[1536,16]{1,0:T(8,128)(2,1)} %get-tuple-element.5), channel_id=1, source_target_pairs={{0,16},{16,32},{32,48},{48,64},{64,80},{80,96},{96,112},{112,128},... | collective-permute-start | bytes 147464 | tf_op jit(solution)/shard_map/ppermute | solution.py:22
  84.8 12.9 %collective-permute-start.1 = (bf16[1536,16]{1,0:T(8,128)(2,1)}, bf16[1536,16]{1,0:T(8,128)(2,1)}, u32[]{:S(2)}, u32[]{:S(2)}) collective-permute-start(bf16[1536,16]{1,0:T(8,128)(2,1)} %get-tuple-element.4), channel_id=1, source_target_pairs={{16,0},{32,16},{48,32},{64,48},{80,64},{96,80},{112,96},{128,112},... | collective-permute-start | bytes 147464 | tf_op jit(solution)/shard_map/ppermute | solution.py:24
  104.4 3.1 %copy-start.1 = (bf16[1536,1056]{1,0:T(8,128)(2,1)S(1)}, bf16[1536,1056]{1,0:T(8,128)(2,1)}, u32[]{:S(2)}) copy-start(bf16[1536,1056]{1,0:T(8,128)(2,1)} %concatenate.21) | copy-start | bytes 9732100
  104.4 3.1 %copy-start.5 = (f32[1536]{0:T(1024)S(1)}, f32[1536]{0:T(1024)}, u32[]{:S(2)}) copy-start(f32[1536]{0:T(1024)} %param.11) | copy-start | bytes 18436
  107.4 3.7 %copy-start.4 = (bf16[5,96,1536]{2,1,0:T(8,128)(2,1)S(1)}, bf16[5,96,1536]{2,1,0:T(8,128)(2,1)}, u32[]{:S(2)}) copy-start(bf16[5,96,1536]{2,1,0:T(8,128)(2,1)} %param.9) | copy-start | bytes 4423684
  113.4 2.3 %copy-start.2 = (bf16[96,1024]{1,0:T(8,128)(2,1)S(1)}, bf16[96,1024]{1,0:T(8,128)(2,1)}, u32[]{:S(2)}) copy-start(bf16[96,1024]{1,0:T(8,128)(2,1)} %param.8) | copy-start | bytes 589828
  113.4 2.3 %copy-start.6 = (f32[96]{0:T(128)S(1)}, f32[96]{0:T(128)}, u32[]{:S(2)}) copy-start(f32[96]{0:T(128)} %param.10) | copy-start | bytes 1156
  115.8 80.9 %copy-start.7 = (bf16[64,32,128]{2,1,0:T(8,128)(2,1)S(1)}, bf16[64,32,128]{2,1,0:T(8,128)(2,1)}, u32[]{:S(2)}) copy-start(bf16[64,32,128]{2,1,0:T(8,128)(2,1)} %param.13) | copy-start | bytes 1572868
  115.8 80.9 %copy-start.8 = (f32[128]{0:T(128)S(1)}, f32[128]{0:T(128)}, u32[]{:S(2)}) copy-start(f32[128]{0:T(128)} %param.15) | copy-start | bytes 1540
  116.5 82.2 %copy-start.3 = (bf16[96,1024]{1,0:T(8,128)(2,1)}, bf16[96,1024]{1,0:T(8,128)(2,1)S(1)}, u32[]{:S(2)}) copy-start(bf16[96,1024]{1,0:T(8,128)(2,1)S(1)} %fusion.47) | copy-start | bytes 589828
  180.4 3.1 %collective-permute-start.2 = (bf16[64,32]{0,1:T(8,128)(2,1)S(1)}, bf16[64,32]{0,1:T(8,128)(2,1)S(1)}, u32[]{:S(2)}, u32[]{:S(2)}) collective-permute-start(bf16[64,32]{0,1:T(8,128)(2,1)S(1)} %get-tuple-element.7), channel_id=1, source_target_pairs={{0,16},{16,0},{32,48},{48,32},{64,80},{80,64},{96,112},{112,96},{1... | collective-permute-start | bytes 12296 | tf_op jit(solution)/shard_map/ppermute | solution.py:38
  183.5 7.0 %collective-permute-start.3 = (bf16[128,32]{0,1:T(8,128)(2,1)S(1)}, bf16[128,32]{0,1:T(8,128)(2,1)S(1)}, u32[]{:S(2)}, u32[]{:S(2)}) collective-permute-start(bf16[128,32]{0,1:T(8,128)(2,1)S(1)} %maximum_select_fusion.1), channel_id=1, source_target_pairs={{0,32},{32,0},{16,48},{48,16},{64,96},{96,64},{80,112},{112,80},{1... | collective-permute-start | bytes 24584 | tf_op jit(solution)/shard_map/ppermute | solution.py:38
  190.6 5.6 %collective-permute-start.4 = (bf16[256,32]{0,1:T(8,128)(2,1)S(1)}, bf16[256,32]{0,1:T(8,128)(2,1)S(1)}, u32[]{:S(2)}, u32[]{:S(2)}) collective-permute-start(bf16[256,32]{0,1:T(8,128)(2,1)S(1)} %maximum_select_fusion), channel_id=1, source_target_pairs={{0,64},{64,0},{16,80},{80,16},{32,96},{96,32},{48,112},{112,48},{1... | collective-permute-start | bytes 49160 | tf_op jit(solution)/shard_map/ppermute | solution.py:38
